TPU v7x, 32 devices: a whole 2x2x4 slice. The times are simulated.
32 devices in a mesh: groups: 2 (over x), dp: 16 (over z, y, core).
Axes of the slice: x: 2, y: 2, z: 4, core: 2. Of those that a mesh axis runs over, the one named last changes fastest.
Arguments:
- gate_preact: bfloat16 [1024, 28672], P('groups', 'dp'), parts along dimension 0, may hold values from -6 to 6
- up_preact: bfloat16 [1024, 28672], P('groups', 'dp'), parts along dimension 0, may hold values from -6 to 6
- out_grad: bfloat16 [1024, 8192], P(('groups', 'dp')), parts along dimension 0, may hold values from -6 to 6
- layer_input: bfloat16 [1024, 8192], P('groups', 'dp'), parts along dimension 0, may hold values from -6 to 6
- w_down: bfloat16 [28672, 8192], P('dp'), may hold values from -0.03125 to 0.03125
- proj_in_down: bfloat16 [64, 28672], P(None, 'dp'), may hold values from -0.03125 to 0.03125
- proj_out_down: bfloat16 [64, 8192], replicated, may hold values from -0.0625 to 0.0625
- proj_in_up: bfloat16 [64, 8192], P(None, 'dp'), may hold values from -0.0625 to 0.0625
- proj_out_up: bfloat16 [64, 28672], P(None, 'dp'), may hold values from -0.03125 to 0.03125
- queries: bfloat16 [2048, 8192], P('dp'), may hold values from -0.005859375 to 0.005859375
Outputs:
- scores: float32 [8, 2048], P('groups', 'dp'), parts along dimension 0
There are 2 independent parts, one for each index of `groups`. A program takes and returns all parts, laid end to end along the dimension named above; an argument that names none is the same for every part. Nothing has to cross between parts.
All inputs are finite; a program needn't handle non-finite values.
Results may differ from a plain program's by a relative error of at most 0.0048.
Values may be sent and summed in bfloat16 or wider, within the bound.
A program may use at most 128 MiB of HBM per device.

v0:
```python
import jax
import jax.numpy as jnp
from jax import lax
from jax.sharding import PartitionSpec as P

SEQ_LEN = 128


def outer_sums(left, right):
    examples = left.shape[0] // SEQ_LEN
    left_f = left.reshape(examples, SEQ_LEN, left.shape[1])
    right_f = right.reshape(examples, SEQ_LEN, right.shape[1])
    summed = jnp.einsum("elk,elj->ekj", left_f, right_f, precision=lax.Precision.HIGHEST)
    return summed.reshape(examples, left.shape[1] * right.shape[1])


def shards(
    gate_preact,
    up_preact,
    out_grad,
    layer_input,
    w_down,
    proj_in_down,
    proj_out_down,
    proj_in_up,
    proj_out_up,
    queries,
):
    swished = jax.nn.silu(gate_preact.astype(jnp.float32))
    hidden = (swished * up_preact.astype(jnp.float32)).astype(jnp.bfloat16)
    in_down = jnp.dot(hidden, proj_in_down.T, preferred_element_type=jnp.float32)
    sketch_side = proj_out_down.shape[0]
    piece = lax.all_gather(out_grad, "dp", axis=0, tiled=True)
    down_rounded = jnp.dot(piece, proj_out_down.T, preferred_element_type=jnp.float32).astype(
        jnp.bfloat16
    )
    down_rounded = lax.optimization_barrier(down_rounded).astype(jnp.float32)
    grad_rows_here = jnp.dot(piece, w_down.T, preferred_element_type=jnp.float32)
    grad_up = (grad_rows_here * swished).astype(jnp.bfloat16)
    up_rows = jnp.dot(grad_up, proj_out_up.T, preferred_element_type=jnp.float32)
    projected = jnp.concatenate([down_rounded, up_rows], axis=1)
    out_down = projected[:, :sketch_side]
    out_up = projected[:, sketch_side:]
    whole_input, whole_proj = (
        lax.all_gather(layer_input, "dp", axis=1, tiled=True),
        lax.all_gather(proj_in_up, "dp", axis=1, tiled=True),
    )
    in_up = jnp.dot(whole_input, whole_proj.T, preferred_element_type=jnp.float32)
    partial_sketch = jnp.concatenate(
        [outer_sums(out_down, in_down), outer_sums(out_up, in_up)], axis=1
    )
    sketches = lax.psum(partial_sketch, "dp").astype(jnp.bfloat16)
    return jnp.dot(sketches, queries.T, preferred_element_type=jnp.float32)


def solution(mesh):
    in_specs = (
        P("groups", "dp"),
        P("groups", "dp"),
        P(("groups", "dp"), None),
        P("groups", "dp"),
        P("dp", None),
        P(None, "dp"),
        P(),
        P(None, "dp"),
        P(None, "dp"),
        P("dp", None),
    )
    out_specs = P("groups", "dp")
    return jax.shard_map(shards, mesh=mesh, in_specs=in_specs, out_specs=out_specs, check_vma=False)
```

profile of v0, /device:TPU:0, one launch (start us, length us, event | category | flops | bytes accessed | tf_op | source)
XLA Modules:
  0.0 306.9 jit_solution(3847258788149241289)
XLA Ops:
  6.5 0.0 copy-start
  6.5 0.0 all-gather.8.cloned.1.call-start
  6.5 0.7 all-gather.8.cloned.1.call-update
  7.3 0.0 all-gather.6.cloned.1.call-start
  7.3 0.7 all-gather.6.cloned.1.call-update
  8.0 0.0 all-gather.4.cloned.1.call-start
  8.1 0.7 all-gather.4.cloned.1.call-update
  8.7 4.0 %fusion.5 = f32[8,4,8,128]{3,2,1,0:T(8,128)} fusion(bf16[64,1792]{1,0:T(8,128)(2,1)} %param.15, bf16[512,1792]{1,0:T(8,128)(2,1)} %param.11, bf16[512,1792]{1,0:T(8,128)(2,1)} %param.10), kind=kOutput, calls=%fused_computation.9 | convolution fusion | flops 124780544 | bytes 4030464 | tf_op jit(solution)/shard_map/dot_general | solution.py:31
  12.7 36.3 %all-gather.8.cloned.1.call-done = bf16[64,8192]{1,0:T(8,128)(2,1)} async-done(((bf16[64,512]{1,0:T(8,128)(2,1)}), bf16[64,8192]{1,0:T(8,128)(2,1)}) %all-gather.8.cloned.1.call-update) | async-done | bytes 1048592 | tf_op jit(solution)/shard_map/all_gather | solution.py:46
  49.1 79.8 %all-gather.6.cloned.1.call-done = bf16[512,8192]{1,0:T(8,128)(2,1)} async-done(((bf16[512,512]{1,0:T(8,128)(2,1)}), bf16[512,8192]{1,0:T(8,128)(2,1)}) %all-gather.6.cloned.1.call-update) | async-done | bytes 8388624 | tf_op jit(solution)/shard_map/all_gather | solution.py:45
  128.8 6.3 %convolution_bitcast_fusion = f32[8,4,8,128]{3,2,1,0:T(8,128)S(1)} fusion(bf16[512,8192]{1,0:T(8,128)(2,1)} %all-gather.6.cloned.1.call-done, bf16[64,8192]{1,0:T(8,128)(2,1)} %all-gather.8.cloned.1.call-done), kind=kOutput, calls=%fused_computation.11 | convolution fusion | flops 536870912 | bytes 9568256 | tf_op jit(solution)/shard_map/dot_general | solution.py:48
  135.1 0.0 copy-start.1
  135.1 69.0 %all-gather.4.cloned.1.call-done = bf16[512,8192]{1,0:T(8,128)(2,1)} async-done(((bf16[32,8192]{1,0:T(8,128)(2,1)}), bf16[512,8192]{1,0:T(8,128)(2,1)}) %all-gather.4.cloned.1.call-update) | async-done | bytes 8388624 | tf_op jit(solution)/shard_map/all_gather | solution.py:33
  204.1 28.2 %fusion.6 = f32[8,4,8,128]{3,2,1,0:T(8,128)S(1)} fusion(bf16[64,1792]{1,0:T(8,128)(2,1)} %param.18, bf16[512,8192]{1,0:T(8,128)(2,1)} %all-gather.4.cloned.1.call-done, bf16[1792,8192]{1,0:T(8,128)(2,1)} %param.14, bf16[512,1792]{1,0:T(8,128)(2,1)} %param.10), kind=kOutput, calls=%fused_computation.10 | convolution fusion | flops 15156248576 | bytes 39944192 | tf_op jit(solution)/shard_map/dot_general | solution.py:40
  232.3 0.3 fusion.7
  232.7 0.1 reshape.23
  232.8 0.0 copy-done.1
  232.8 0.0 copy-start.2
  232.8 6.1 %convolution_convert_fusion = bf16[512,64]{0,1:T(8,128)(2,1)S(1)} fusion(bf16[512,8192]{1,0:T(8,128)(2,1)} %all-gather.4.cloned.1.call-done, bf16[64,8192]{1,0:T(8,128)(2,1)S(1)} %copy-done.1), kind=kOutput, calls=%fused_computation.12 | convolution fusion | flops 536903680 | bytes 9502720 | tf_op jit(solution)/shard_map/dot_general | solution.py:34
  238.9 0.0 copy-done.2
  238.9 0.2 fusion.12
  239.1 0.1 reshape.20
  239.3 59.8 %all-reduce.1 = bf16[4,8192]{1,0:T(4,128)(2,1)S(1)} all-reduce(f32[4,8192]{1,0:T(4,128)S(1)} %pad_maximum_fusion), channel_id=1, replica_groups=mesh['groups'=2,'dp'=16] {'dp'}, use_global_device_ids=true, to_apply=%region_0.1 | all-reduce | flops 32768 | bytes 196608 | tf_op jit(solution)/shard_map/psum | solution.py:52
  299.1 0.0 copy-done
  299.1 1.2 fusion.21
  (1 shorter events, 0.0 us)
Async XLA Ops:
  6.5 292.6 %copy-start = (bf16[128,8192]{1,0:T(8,128)(2,1)S(1)}, bf16[128,8192]{1,0:T(8,128)(2,1)}, u32[]{:S(2)}) copy-start(bf16[128,8192]{1,0:T(8,128)(2,1)} %param.19) | copy-start | bytes 6291460
  6.5 42.5 %all-gather.8.cloned.1.call-start = ((), (), s32[]{:S(2)}) async-start(), calls=%async_computation.2 | async-start | bytes 1114112 | tf_op jit(solution)/shard_map/all_gather | solution.py:46
  7.3 121.6 %all-gather.6.cloned.1.call-start = ((), (), s32[]{:S(2)}) async-start(), calls=%async_computation.1 | async-start | bytes 8912896 | tf_op jit(solution)/shard_map/all_gather | solution.py:45
  8.0 196.1 %all-gather.4.cloned.1.call-start = ((), (), s32[]{:S(2)}) async-start(), calls=%async_computation | async-start | bytes 8912896 | tf_op jit(solution)/shard_map/all_gather | solution.py:33
  135.1 97.7 %copy-start.1 = (bf16[64,8192]{1,0:T(8,128)(2,1)S(1)}, bf16[64,8192]{1,0:T(8,128)(2,1)}, u32[]{:S(2)}) copy-start(bf16[64,8192]{1,0:T(8,128)(2,1)} %param.16) | copy-start | bytes 3145732
  232.8 6.1 %copy-start.2 = (f32[8,4,8,128]{3,2,1,0:T(8,128)S(1)}, f32[8,4,8,128]{3,2,1,0:T(8,128)}, u32[]{:S(2)}) copy-start(f32[8,4,8,128]{3,2,1,0:T(8,128)} %fusion.5) | copy-start | bytes 393220
Sparse Core Ops, SparseCore 0:
  9.5 39.4 all-gather.7
  51.2 77.5 all-gather.5
  131.0 73.0 all-gather.3
where the time goes:
time: 307 us
  waiting for transfers between devices  187 us (61%)
  blocking collectives  59.8 us (19%)
  matrix products  46.3 us (15%)
  between operations  13.2 us (4%)
    all_gather x1, waiting for transfers between devices, shards(): lax.all_gather(layer_input, 'dp', axis=1, tiled=True)  79.8 us
    all_gather x1, waiting for transfers between devices, shards(): piece = lax.all_gather(out_grad, 'dp', axis=0, tiled=True)  69 us
    psum x1, blocking collectives, shards(): sketches = lax.psum(partial_sketch, 'dp').astype(jnp.bfloat16)  59.8 us
    all_gather x1, waiting for transfers between devices, shards(): lax.all_gather(proj_in_up, 'dp', axis=1, tiled=True)  36.3 us
    dot_general x1, matrix products, shards(): jnp.dot(grad_up, proj_out_up.T, preferred_element_type=jnp.float32)  28.2 us
    dot_general x1, matrix products, shards(): jnp.dot(whole_input, whole_proj.T, preferred_element_type=jnp.float32)  6.27 us
  transfers between devices with their start and end apart: 3, of which 3 were waited for; matrix products, arithmetic and copies ran while one was open for 3% of the time, Pallas kernels for 0%

commit v1 on v0

v1 whole, which is shorter than its diff:
```python
import functools

import jax
import jax.numpy as jnp
from jax import lax
from jax.experimental import pallas as pl
from jax.experimental.pallas import tpu as pltpu
from jax.sharding import PartitionSpec as P

SEQ_LEN = 128
F32 = jnp.float32
BF16 = jnp.bfloat16
MESH = pl.DeviceIdType.MESH
HIGHEST = lax.Precision.HIGHEST

CHUNKS = 16
AHEAD = 4
NZ = 4
NDEV = 16
NB = 256


def y_first(chunk):
    return chunk % 5 == 2


def nt(a, b, precision=None):
    return lax.dot_general(
        a, b, (((1,), (1,)), ((), ())), precision=precision, preferred_element_type=F32
    )


def kernel(
    gate_h, up_h, og_h, li_h, w_h, pid_h, pod_h, piu_h, pou_h, q_h,
    out_ref,
    og, w, pod, gate, up, sw, acc, li, piu, pid, pou, qv, odt, ind, iup, rs1, ag1, skp, rs2, tmp, g16, g32,
    own_sem, w_sem, gu_sem, misc_sem, q_sem,
    core_s, core_r, y_s, y_r, up_s, dn_s, zb_r, za_r,
    a2a_s, a2a_r,
):
    rows, width = og_h.shape[0], og.shape[2]
    nblocks = gate.shape[0]
    me = lax.axis_index("dp")
    z, y, core = me // 4, (me // 2) % 2, me % 2
    above, below = me + 4, me - 4
    ypeer = me + 2 - 4 * y
    sibling = me + 1 - 2 * core

    def row(zz, yy):
        return pl.ds(pl.multiple_of((zz * 4 + yy * 2 + core) * rows, rows), rows)

    def push(chunk, where, to, send, recv):
        pltpu.make_async_remote_copy(
            src_ref=og.at[chunk, where], dst_ref=og.at[chunk, where],
            send_sem=send, recv_sem=recv, device_id={"dp": to}, device_id_type=MESH,
        ).start()

    def settle(ref, sem):
        pltpu.make_async_copy(ref, ref, sem).wait()

    def to_core(chunk, where):
        push(chunk, where, sibling, core_s.at[chunk], core_r.at[chunk])

    def to_y(chunk, where):
        push(chunk, where, ypeer, y_s.at[chunk], y_r.at[chunk])

    def to_above(chunk, where, dist):
        @pl.when(z < NZ - 1)
        def _():
            push(chunk, where, above, up_s.at[chunk], zb_r.at[chunk, dist])

    def to_below(chunk, where, dist):
        @pl.when(z > 0)
        def _():
            push(chunk, where, below, dn_s.at[chunk], za_r.at[chunk, dist])

    def everyone(fn):
        def one(k, _):
            fn(lax.rem(me + k, NDEV))
            return 0
        lax.fori_loop(1, NDEV, one, 0)

    def send_all(stage, src_of, dst):
        def one(p):
            pltpu.make_async_remote_copy(
                src_ref=src_of(p), dst_ref=dst.at[me],
                send_sem=a2a_s.at[stage], recv_sem=a2a_r.at[stage],
                device_id={"dp": p}, device_id_type=MESH,
            ).start()
        everyone(one)

    def got_all(stage, dst):
        settle(dst.at[pl.ds(0, NDEV - 1)], a2a_r.at[stage])

    mine = row(z, y)
    for c in range(CHUNKS):
        pltpu.make_async_copy(og_h.at[:, pl.ds(c * width, width)], og.at[c, mine], own_sem).start()
    pltpu.make_async_copy(li_h, li, misc_sem.at[0]).start()
    pltpu.make_async_copy(piu_h, piu, misc_sem.at[1]).start()

    barrier = pltpu.get_barrier_semaphore()
    everyone(lambda p: pl.semaphore_signal(barrier, inc=1, device_id={"dp": p}, device_id_type=MESH))

    settle(og.at[0], own_sem)
    pl.semaphore_wait(barrier, NDEV - 1)

    def send_own(c):
        to_above(c, mine, 0)
        to_below(c, mine, 0)
        to_y(c, mine)
        to_core(c, mine)

    lax.fori_loop(0, AHEAD, lambda c, _: (send_own(c), 0)[1], 0)

    for n in range(nblocks):
        cols = pl.ds(n * NB, NB)
        pltpu.make_async_copy(gate_h.at[:, cols], gate.at[n], gu_sem.at[n]).start()
        pltpu.make_async_copy(up_h.at[:, cols], up.at[n], gu_sem.at[nblocks + n]).start()
        pltpu.make_async_copy(pid_h.at[:, cols], pid.at[n], misc_sem.at[2]).start()
        pltpu.make_async_copy(pou_h.at[:, cols], pou.at[n], misc_sem.at[3]).start()
    for c in range(CHUNKS):
        cols = pl.ds(c * width, width)
        pltpu.make_async_copy(w_h.at[:, cols], w.at[c], w_sem.at[c]).start()
        pltpu.make_async_copy(pod_h.at[:, cols], pod.at[c], w_sem.at[CHUNKS + c]).start()
    pltpu.make_async_copy(q_h, qv, q_sem).start()

    settle(li, misc_sem.at[0])
    settle(piu, misc_sem.at[1])
    twice = jnp.concatenate([piu[...], piu[...]], axis=0)
    part = nt(li[...], twice)
    half = part.shape[0] // 2
    lane = lax.broadcasted_iota(jnp.int32, (half, 128), 1)
    packed = jnp.where(lane < 64, part[:half], part[half:])
    iup[...] = packed.reshape(iup.shape)
    send_all(0, lambda p: iup.at[p], rs1)
    rs1[me] = iup[me]

    acc[...] = jnp.zeros_like(acc)
    odt[...] = jnp.zeros_like(odt)
    ind[...] = jnp.zeros_like(ind)
    settle(pid, misc_sem.at[2])
    settle(pou, misc_sem.at[3])

    def hidden_block(n):
        settle(gate.at[n], gu_sem.at[n])
        settle(up.at[n], gu_sem.at[nblocks + n])
        v = gate[n].astype(F32)
        s = v / (1.0 + jnp.exp(-v))
        sw[n] = s
        hidden = (s * up[n].astype(F32)).astype(BF16)
        pid2 = jnp.concatenate([pid[n], pid[n]], axis=0)
        ind[...] += nt(hidden, pid2)

    def z_stage(c, d):
        first = y_first(c)

        @pl.when(z >= d)
        def _():
            @pl.when(jnp.logical_not(first))
            def _():
                here = row(z - d, y)
                settle(og.at[c, here], zb_r.at[c, d - 1])
                if d < NZ - 1:
                    to_above(c, here, d)
                to_y(c, here)
                to_core(c, here)

            @pl.when(first)
            def _():
                settle(og.at[c, pl.ds(0, 2 * rows)], zb_r.at[c, d - 1])
                for yy in range(2):
                    here = row(z - d, yy)
                    if d < NZ - 1:
                        to_above(c, here, d)
                    to_core(c, here)

        @pl.when(z + d < NZ)
        def _():
            @pl.when(jnp.logical_not(first))
            def _():
                here = row(z + d, y)
                settle(og.at[c, here], za_r.at[c, d - 1])
                if d < NZ - 1:
                    to_below(c, here, d)
                to_y(c, here)
                to_core(c, here)

            @pl.when(first)
            def _():
                settle(og.at[c, pl.ds(0, 2 * rows)], za_r.at[c, d - 1])
                for yy in range(2):
                    here = row(z + d, yy)
                    if d < NZ - 1:
                        to_below(c, here, d)
                    to_core(c, here)

    def y_early(c):
        @pl.when(y_first(c))
        def _():
            here = row(z, 1 - y)
            settle(og.at[c, here], y_r.at[c])
            to_above(c, here, 0)
            to_below(c, here, 0)
            to_core(c, here)

    def y_late(c):
        @pl.when(jnp.logical_not(y_first(c)))
        def _():
            settle(og.at[c, pl.ds(0, NZ * rows)], y_r.at[c])
            for zz in range(NZ):
                to_core(c, row(zz, 1 - y))

    def arrived(c):
        settle(og.at[c, pl.ds(0, 8 * rows)], core_r.at[c])
        settle(w.at[c], w_sem.at[c])
        settle(pod.at[c], w_sem.at[CHUNKS + c])

    def multiply(c):
        arrived(c)

        def one(n, _):
            units = pl.ds(pl.multiple_of(n * NB, NB), NB)
            acc[n] += nt(og[c], w[c, units, :])
            return 0

        lax.fori_loop(0, nblocks, one, 0)
        odt[...] += nt(pod[c], og[c])

    def within(c, fn):
        @pl.when(jnp.logical_and(c >= 0, c < CHUNKS))
        def _():
            fn(c)

    def step(t, _):
        within(t + AHEAD, send_own)
        within(t, y_early)
        within(t, lambda c: z_stage(c, 1))
        within(t - 1, lambda c: z_stage(c, 2))
        within(t - 2, lambda c: z_stage(c, 3))
        within(t - 3, y_late)

        @pl.when(t < nblocks)
        def _():
            hidden_block(t)

        @pl.when(t == 2)
        def _():
            got_all(0, rs1)
            ag1[me] = jnp.sum(rs1[...], axis=0)
            send_all(1, lambda p: ag1.at[me], ag1)

        @pl.when(t >= 4)
        def _():
            multiply(t - 4)

        return 0

    lax.fori_loop(0, CHUNKS + 3, step, 0)

    last = CHUNKS - 1
    got_all(1, ag1)
    arrived(last)

    def finish(n, out_up):
        units = pl.ds(pl.multiple_of(n * NB, NB), NB)
        grad = acc[n] + nt(og[last], w[last, units, :])
        return out_up + nt(pou[n], (grad * sw[n]).astype(BF16))

    out_up = lax.fori_loop(0, nblocks, finish, jnp.zeros(odt.shape, F32))
    out_down = (odt[...] + nt(pod[last], og[last])).astype(BF16).astype(F32)

    examples = out_up.shape[1] // SEQ_LEN
    in_up = ag1[...].reshape(half, 128)
    lane = lax.broadcasted_iota(jnp.int32, (64, 128), 1)
    for e in range(examples):
        toks = slice(e * SEQ_LEN, (e + 1) * SEQ_LEN)
        at = (e * SEQ_LEN) % half
        down = jnp.dot(out_down[:, toks], ind[toks, :], precision=HIGHEST, preferred_element_type=F32)
        ups = jnp.dot(out_up[:, toks], in_up[at:at + SEQ_LEN], precision=HIGHEST, preferred_element_type=F32)
        if e * SEQ_LEN < half:
            ups = pltpu.roll(ups, 64, 1)
        both = jnp.where(lane < 64, down, ups)
        skp[pl.ds(e * 4, 4)] = both.reshape(4, 16, 128)

    send_all(2, lambda p: skp.at[p], rs2)
    rs2[me] = skp[me]
    got_all(2, rs2)
    tmp[...] = jnp.sum(rs2[...], axis=0)
    even = tmp[pl.ds(0, 8, stride=2), :]
    odd = tmp[pl.ds(1, 8, stride=2), :]
    lane = lax.broadcasted_iota(jnp.int32, (8, 128), 1)
    down = jnp.where(lane < 64, even, pltpu.roll(odd, 64, 1))
    ups = jnp.where(lane < 64, pltpu.roll(even, 64, 1), odd)
    g16[me] = jnp.concatenate([down, ups], axis=0).astype(BF16)
    send_all(3, lambda p: g16.at[me], g16)
    settle(qv, q_sem)
    got_all(3, g16)
    g32[...] = g16[...].astype(F32).reshape(g32.shape)
    parts = []
    for half_at in (0, 8):
        for quarter in range(4):
            for r in range(8):
                parts.append(g32[:, quarter, half_at + r, :])
    sketches = jnp.concatenate(parts, axis=1).astype(BF16)
    out_ref[...] = nt(sketches, qv[...])

    def drained(c, _):
        settle(og.at[c, pl.ds(0, 8 * rows)], core_s.at[c])
        first = y_first(c)

        @pl.when(first)
        def _():
            settle(og.at[c, pl.ds(0, rows)], y_s.at[c])

        @pl.when(jnp.logical_not(first))
        def _():
            settle(og.at[c, pl.ds(0, NZ * rows)], y_s.at[c])

        for k in range(NZ - 1):
            for wide in (False, True):
                size = pl.ds(0, (k + 1) * rows * (2 if wide else 1))
                same = first if wide else jnp.logical_not(first)

                @pl.when(jnp.logical_and(same, z == k))
                def _():
                    settle(og.at[c, size], up_s.at[c])

                @pl.when(jnp.logical_and(same, z == NZ - 1 - k))
                def _():
                    settle(og.at[c, size], dn_s.at[c])
        return 0

    lax.fori_loop(0, CHUNKS, drained, 0)
    for stage, dst in enumerate((rs1, ag1, rs2, g16)):
        settle(dst.at[pl.ds(0, NDEV - 1)], a2a_s.at[stage])


def fused(gate, up, out_grad, layer_input, w_down, pid, pod, piu, pou, queries):
    tokens, units = gate.shape
    rows, features = out_grad.shape
    width = features // CHUNKS
    nblocks = units // NB
    examples = tokens // SEQ_LEN
    dma = pltpu.SemaphoreType.DMA
    scratch = [
        pltpu.VMEM((CHUNKS, tokens, width), BF16),
        pltpu.VMEM((CHUNKS, units, width), BF16),
        pltpu.VMEM((CHUNKS, 64, width), BF16),
        pltpu.VMEM((nblocks, tokens, NB), BF16),
        pltpu.VMEM((nblocks, tokens, NB), BF16),
        pltpu.VMEM((nblocks, tokens, NB), F32),
        pltpu.VMEM((nblocks, tokens, NB), F32),
        pltpu.VMEM(layer_input.shape, BF16),
        pltpu.VMEM(piu.shape, BF16),
        pltpu.VMEM((nblocks, 64, NB), BF16),
        pltpu.VMEM((nblocks, 64, NB), BF16),
        pltpu.VMEM(queries.shape, BF16),
        pltpu.VMEM((64, tokens), F32),
        pltpu.VMEM((tokens, 128), F32),
        pltpu.VMEM((NDEV, 16, 128), F32),
        pltpu.VMEM((NDEV, 16, 128), F32),
        pltpu.VMEM((NDEV, 16, 128), F32),
        pltpu.VMEM((NDEV, 16, 128), F32),
        pltpu.VMEM((NDEV, 16, 128), F32),
        pltpu.VMEM((16, 128), F32),
        pltpu.VMEM((NDEV, 16, 128), BF16),
        pltpu.VMEM((examples, 4, 16, 128), F32),
        dma, dma((2 * CHUNKS,)), dma((2 * nblocks,)), dma((4,)), dma,
        dma((CHUNKS,)), dma((CHUNKS,)), dma((CHUNKS,)), dma((CHUNKS,)),
        dma((CHUNKS,)), dma((CHUNKS,)), dma((CHUNKS, NZ - 1)), dma((CHUNKS, NZ - 1)),
        dma((4,)), dma((4,)),
    ]
    return pl.pallas_call(
        kernel,
        out_shape=jax.ShapeDtypeStruct((examples, queries.shape[0]), F32),
        in_specs=[pl.BlockSpec(memory_space=pl.ANY)] * 10,
        out_specs=pl.BlockSpec(memory_space=pltpu.VMEM),
        scratch_shapes=scratch,
        compiler_params=pltpu.CompilerParams(
            collective_id=0, has_side_effects=True, vmem_limit_bytes=60 * 1024 * 1024
        ),
        cost_estimate=pl.CostEstimate(
            flops=2 * tokens * units * features, bytes_accessed=2 * units * features, transcendentals=tokens * units
        ),
    )(gate, up, out_grad, layer_input, w_down, pid, pod, piu, pou, queries)


def outer_sums(left, right):
    examples = left.shape[0] // SEQ_LEN
    left_f = left.reshape(examples, SEQ_LEN, left.shape[1])
    right_f = right.reshape(examples, SEQ_LEN, right.shape[1])
    summed = jnp.einsum("elk,elj->ekj", left_f, right_f, precision=HIGHEST)
    return summed.reshape(examples, left.shape[1] * right.shape[1])


def general(gate, up, out_grad, layer_input, w_down, pid, pod, piu, pou, queries):
    swished = jax.nn.silu(gate.astype(F32))
    hidden = (swished * up.astype(F32)).astype(BF16)
    in_down = nt(hidden, pid)
    in_up = lax.psum(nt(layer_input, piu), "dp")
    piece = lax.all_gather(out_grad, "dp", axis=0, tiled=True)
    out_down = lax.optimization_barrier(nt(piece, pod).astype(BF16)).astype(F32)
    grad_up = (nt(piece, w_down) * swished).astype(BF16)
    out_up = nt(grad_up, pou)
    partial_sketch = jnp.concatenate([outer_sums(out_down, in_down), outer_sums(out_up, in_up)], axis=1)
    sketches = lax.psum(partial_sketch, "dp").astype(BF16)
    return nt(sketches, queries)


def solution(mesh):
    in_specs = (
        P("groups", "dp"),
        P("groups", "dp"),
        P(("groups", "dp"), None),
        P("groups", "dp"),
        P("dp", None),
        P(None, "dp"),
        P(),
        P(None, "dp"),
        P(None, "dp"),
        P("dp", None),
    )
    out_specs = P("groups", "dp")
    body = fused if mesh.shape["dp"] == NDEV else general
    return jax.shard_map(body, mesh=mesh, in_specs=in_specs, out_specs=out_specs, check_vma=False)
```

time: 307 us -> 108 us (0.35)
  waiting for transfers between devices: 187 us -> 0 us
  Pallas kernels: 0 us -> 107 us
  blocking collectives: 59.8 us -> 0 us
  matrix products: 46.3 us -> 0 us
  between operations: 13.2 us -> 0.01 us
    all_gather x3 -> x0, waiting for transfers between devices: 185 us -> none  [the longest x1 79.8 us: shards(): lax.all_gather(layer_input, 'dp', axis=1, tiled=True)]
    pallas_call x0 -> x1, Pallas kernels: none -> 107 us  [fused(): pl.pallas_call(kernel, out_shape=jax.ShapeDtypeStruct((examples, queries....]
    psum x1 -> x0, blocking collectives: 59.8 us -> none  [shards(): sketches = lax.psum(partial_sketch, 'dp').astype(jnp.bfloat16)]
    dot_general x7 -> x0, matrix products: 46.3 us -> none  [the longest x1 28.2 us: shards(): jnp.dot(grad_up, proj_out_up.T, preferred_element_type=jnp.float32)]
  transfers between devices with their start and end apart: 3 -> 0, of which waited for: 3 -> 0; matrix products, arithmetic and copies ran while one was open for 3% -> 0% of each run, Pallas kernels for 0% -> 0%
where the time goes in v1:
time: 108 us
  Pallas kernels  107 us (99%)
  local copies, waits for them, and re-layouts  1.26 us (1%)
    pallas_call x1, Pallas kernels, fused(): pl.pallas_call(kernel, out_shape=jax.ShapeDtypeStruct((examples, queries....  107 us

profile of v1, /device:TPU:0, one launch (start us, length us, event | category | flops | bytes accessed | tf_op | source)
XLA Modules:
  0.0 108.0 jit_solution(3098225117288606445)
XLA Ops:
  0.0 106.7 %shard_map.100 = f32[4,128]{1,0:T(4,128)} custom-call(bf16[512,1792]{1,0:T(8,128)(2,1)} %gate_h.1, bf16[512,1792]{1,0:T(8,128)(2,1)} %up_h.1, bf16[32,8192]{1,0:T(8,128)(2,1)} %og_h.1, bf16[512,512]{1,0:T(8,128)(2,1)} %li_h.1, bf16[1792,8192]{1,0:T(8,128)(2,1)} %w_h.1, bf16[64,1792]{1,0:T(8,128)(2,1)} %pid_h.1, bf16[64,8192]{1,0:T(8,128)(2,1)} %pod_h.1, ...), custom_call_target="tpu_custom_call" | custom-call | flops 15032385536 | bytes 29360128 | tf_op jit(solution)/shard_map/pallas_call | solution.py:373
  106.7 1.3 %copy.12 = f32[4,128]{1,0:T(4,128)} copy(f32[4,128]{1,0:T(4,128)} %shard_map.100) | data formatting | bytes 4096

commit v2 on v1

--- a/solution.py
+++ b/solution.py
@@ -33,13 +33,14 @@
 def kernel(
     gate_h, up_h, og_h, li_h, w_h, pid_h, pod_h, piu_h, pou_h, q_h,
     out_ref,
-    og, w, pod, gate, up, sw, acc, li, piu, pid, pou, qv, odt, ind, iup, rs1, ag1, skp, rs2, tmp, g16, g32,
+    og, w, gate, up, sw, acc, li, piu, pid, pou, qv, ind, iup, rs1, ag1, skp, rs2, tmp, g16, g32,
     own_sem, w_sem, gu_sem, misc_sem, q_sem,
     core_s, core_r, y_s, y_r, up_s, dn_s, zb_r, za_r,
     a2a_s, a2a_r,
 ):
     rows, width = og_h.shape[0], og.shape[2]
     nblocks = gate.shape[0]
+    side = pod_h.shape[0]
     me = lax.axis_index("dp")
     z, y, core = me // 4, (me // 2) % 2, me % 2
     above, below = me + 4, me - 4
@@ -101,7 +102,7 @@
     barrier = pltpu.get_barrier_semaphore()
     everyone(lambda p: pl.semaphore_signal(barrier, inc=1, device_id={"dp": p}, device_id_type=MESH))
 
-    settle(og.at[0], own_sem)
+    settle(og.at[0, pl.ds(0, CHUNKS * rows)], own_sem)
     pl.semaphore_wait(barrier, NDEV - 1)
 
     def send_own(c):
@@ -120,8 +121,8 @@
         pltpu.make_async_copy(pou_h.at[:, cols], pou.at[n], misc_sem.at[3]).start()
     for c in range(CHUNKS):
         cols = pl.ds(c * width, width)
-        pltpu.make_async_copy(w_h.at[:, cols], w.at[c], w_sem.at[c]).start()
-        pltpu.make_async_copy(pod_h.at[:, cols], pod.at[c], w_sem.at[CHUNKS + c]).start()
+        pltpu.make_async_copy(pod_h.at[:, cols], w.at[c, pl.ds(0, side)], w_sem.at[c]).start()
+        pltpu.make_async_copy(w_h.at[:, cols], w.at[c, pl.ds(side, nblocks * NB)], w_sem.at[c]).start()
     pltpu.make_async_copy(q_h, qv, q_sem).start()
 
     settle(li, misc_sem.at[0])
@@ -136,7 +137,6 @@
     rs1[me] = iup[me]
 
     acc[...] = jnp.zeros_like(acc)
-    odt[...] = jnp.zeros_like(odt)
     ind[...] = jnp.zeros_like(ind)
     settle(pid, misc_sem.at[2])
     settle(pou, misc_sem.at[3])
@@ -146,7 +146,7 @@
         settle(up.at[n], gu_sem.at[nblocks + n])
         v = gate[n].astype(F32)
         s = v / (1.0 + jnp.exp(-v))
-        sw[n] = s
+        sw[n] = s.T
         hidden = (s * up[n].astype(F32)).astype(BF16)
         pid2 = jnp.concatenate([pid[n], pid[n]], axis=0)
         ind[...] += nt(hidden, pid2)
@@ -213,18 +213,11 @@
     def arrived(c):
         settle(og.at[c, pl.ds(0, 8 * rows)], core_r.at[c])
         settle(w.at[c], w_sem.at[c])
-        settle(pod.at[c], w_sem.at[CHUNKS + c])
 
     def multiply(c):
         arrived(c)
 
-        def one(n, _):
-            units = pl.ds(pl.multiple_of(n * NB, NB), NB)
-            acc[n] += nt(og[c], w[c, units, :])
-            return 0
-
-        lax.fori_loop(0, nblocks, one, 0)
-        odt[...] += nt(pod[c], og[c])
+        acc[...] += nt(w[c], og[c])
 
     def within(c, fn):
         @pl.when(jnp.logical_and(c >= 0, c < CHUNKS))
@@ -233,41 +226,40 @@
 
     def step(t, _):
         within(t + AHEAD, send_own)
-        within(t, y_early)
+        within(t + 2, y_early)
         within(t, lambda c: z_stage(c, 1))
-        within(t - 1, lambda c: z_stage(c, 2))
-        within(t - 2, lambda c: z_stage(c, 3))
-        within(t - 3, y_late)
+        within(t - 2, lambda c: z_stage(c, 2))
+        within(t - 4, lambda c: z_stage(c, 3))
+        within(t - 6, y_late)
 
         @pl.when(t < nblocks)
         def _():
             hidden_block(t)
 
-        @pl.when(t == 2)
+        @pl.when(t == 7)
         def _():
             got_all(0, rs1)
             ag1[me] = jnp.sum(rs1[...], axis=0)
             send_all(1, lambda p: ag1.at[me], ag1)
 
-        @pl.when(t >= 4)
-        def _():
-            multiply(t - 4)
+        @pl.when(t >= 8)
+        def _():
+            multiply(t - 8)
 
         return 0
 
-    lax.fori_loop(0, CHUNKS + 3, step, 0)
+    lax.fori_loop(0, CHUNKS + 7, step, 0)
 
     last = CHUNKS - 1
     got_all(1, ag1)
     arrived(last)
 
-    def finish(n, out_up):
-        units = pl.ds(pl.multiple_of(n * NB, NB), NB)
-        grad = acc[n] + nt(og[last], w[last, units, :])
-        return out_up + nt(pou[n], (grad * sw[n]).astype(BF16))
-
-    out_up = lax.fori_loop(0, nblocks, finish, jnp.zeros(odt.shape, F32))
-    out_down = (odt[...] + nt(pod[last], og[last])).astype(BF16).astype(F32)
+    acc[...] += nt(w[last], og[last])
+    out_down = acc[pl.ds(0, side), :].astype(BF16).astype(F32)
+    out_up = jnp.zeros(out_down.shape, F32)
+    for n in range(nblocks):
+        grad = (acc[pl.ds(side + n * NB, NB), :] * sw[n]).astype(BF16)
+        out_up += jnp.dot(pou[n], grad, preferred_element_type=F32)
 
     examples = out_up.shape[1] // SEQ_LEN
     in_up = ag1[...].reshape(half, 128)
@@ -344,18 +336,16 @@
     dma = pltpu.SemaphoreType.DMA
     scratch = [
         pltpu.VMEM((CHUNKS, tokens, width), BF16),
-        pltpu.VMEM((CHUNKS, units, width), BF16),
-        pltpu.VMEM((CHUNKS, 64, width), BF16),
+        pltpu.VMEM((CHUNKS, 64 + units, width), BF16),
         pltpu.VMEM((nblocks, tokens, NB), BF16),
         pltpu.VMEM((nblocks, tokens, NB), BF16),
-        pltpu.VMEM((nblocks, tokens, NB), F32),
-        pltpu.VMEM((nblocks, tokens, NB), F32),
+        pltpu.VMEM((nblocks, NB, tokens), F32),
+        pltpu.VMEM((64 + units, tokens), F32),
         pltpu.VMEM(layer_input.shape, BF16),
         pltpu.VMEM(piu.shape, BF16),
         pltpu.VMEM((nblocks, 64, NB), BF16),
         pltpu.VMEM((nblocks, 64, NB), BF16),
         pltpu.VMEM(queries.shape, BF16),
-        pltpu.VMEM((64, tokens), F32),
         pltpu.VMEM((tokens, 128), F32),
         pltpu.VMEM((NDEV, 16, 128), F32),
         pltpu.VMEM((NDEV, 16, 128), F32),
@@ -365,7 +355,7 @@
         pltpu.VMEM((16, 128), F32),
         pltpu.VMEM((NDEV, 16, 128), BF16),
         pltpu.VMEM((examples, 4, 16, 128), F32),
-        dma, dma((2 * CHUNKS,)), dma((2 * nblocks,)), dma((4,)), dma,
+        dma, dma((CHUNKS,)), dma((2 * nblocks,)), dma((4,)), dma,
         dma((CHUNKS,)), dma((CHUNKS,)), dma((CHUNKS,)), dma((CHUNKS,)),
         dma((CHUNKS,)), dma((CHUNKS,)), dma((CHUNKS, NZ - 1)), dma((CHUNKS, NZ - 1)),
         dma((4,)), dma((4,)),

time: 108 us -> 82.1 us (0.76)
  Pallas kernels: 107 us -> 80.7 us
    pallas_call x1, Pallas kernels: 107 us -> 80.7 us  [fused(): pl.pallas_call(kernel, out_shape=jax.ShapeDtypeStruct((examples, queries....]
where the time goes in v2:
time: 82.1 us; the launch traced here: 82 us
  Pallas kernels  80.7 us (98%)
  local copies, waits for them, and re-layouts  1.26 us (2%)
    pallas_call x1, Pallas kernels, fused(): pl.pallas_call(kernel, out_shape=jax.ShapeDtypeStruct((examples, queries....  80.7 us

profile of v2, /device:TPU:0, one launch (start us, length us, event | category | flops | bytes accessed | tf_op | source)
XLA Modules:
  0.0 82.0 jit_solution(9570494334952558948)
XLA Ops:
  0.0 80.7 %shard_map.100 = f32[4,128]{1,0:T(4,128)} custom-call(bf16[512,1792]{1,0:T(8,128)(2,1)} %gate_h.1, bf16[512,1792]{1,0:T(8,128)(2,1)} %up_h.1, bf16[32,8192]{1,0:T(8,128)(2,1)} %og_h.1, bf16[512,512]{1,0:T(8,128)(2,1)} %li_h.1, bf16[1792,8192]{1,0:T(8,128)(2,1)} %w_h.1, bf16[64,1792]{1,0:T(8,128)(2,1)} %pid_h.1, bf16[64,8192]{1,0:T(8,128)(2,1)} %pod_h.1, ...), custom_call_target="tpu_custom_call" | custom-call | flops 15032385536 | bytes 29360128 | tf_op jit(solution)/shard_map/pallas_call | solution.py:363
  80.7 1.3 %copy.12 = f32[4,128]{1,0:T(4,128)} copy(f32[4,128]{1,0:T(4,128)} %shard_map.100) | data formatting | bytes 4096

commit v3 on v2

--- a/solution.py
+++ b/solution.py
@@ -13,15 +13,15 @@
 MESH = pl.DeviceIdType.MESH
 HIGHEST = lax.Precision.HIGHEST
 
-CHUNKS = 16
-AHEAD = 4
+CHUNKS = 8
+AHEAD = 6
 NZ = 4
 NDEV = 16
 NB = 256
 
 
 def y_first(chunk):
-    return chunk % 5 == 2
+    return chunk % 8 == 4
 
 
 def nt(a, b, precision=None):
@@ -214,10 +214,18 @@
         settle(og.at[c, pl.ds(0, 8 * rows)], core_r.at[c])
         settle(w.at[c], w_sem.at[c])
 
+    def add_product(c):
+        def one(k, _):
+            part = pl.ds(pl.multiple_of(k * 512, 512), 512)
+            acc[...] += nt(w[c, :, part], og[c, :, part])
+            return 0
+
+        lax.fori_loop(0, width // 512, one, 0)
+
     def multiply(c):
         arrived(c)
 
-        acc[...] += nt(w[c], og[c])
+        add_product(c)
 
     def within(c, fn):
         @pl.when(jnp.logical_and(c >= 0, c < CHUNKS))
@@ -228,9 +236,9 @@
         within(t + AHEAD, send_own)
         within(t + 2, y_early)
         within(t, lambda c: z_stage(c, 1))
-        within(t - 2, lambda c: z_stage(c, 2))
-        within(t - 4, lambda c: z_stage(c, 3))
-        within(t - 6, y_late)
+        within(t - 1, lambda c: z_stage(c, 2))
+        within(t - 2, lambda c: z_stage(c, 3))
+        within(t - 3, y_late)
 
         @pl.when(t < nblocks)
         def _():
@@ -242,19 +250,19 @@
             ag1[me] = jnp.sum(rs1[...], axis=0)
             send_all(1, lambda p: ag1.at[me], ag1)
 
-        @pl.when(t >= 8)
-        def _():
-            multiply(t - 8)
+        @pl.when(t >= 4)
+        def _():
+            multiply(t - 4)
 
         return 0
 
-    lax.fori_loop(0, CHUNKS + 7, step, 0)
+    lax.fori_loop(0, CHUNKS + 3, step, 0)
 
     last = CHUNKS - 1
     got_all(1, ag1)
     arrived(last)
 
-    acc[...] += nt(w[last], og[last])
+    add_product(last)
     out_down = acc[pl.ds(0, side), :].astype(BF16).astype(F32)
     out_up = jnp.zeros(out_down.shape, F32)
     for n in range(nblocks):

time: 82.1 us -> 76.5 us (0.932)
  Pallas kernels: 80.7 us -> 75.1 us
    pallas_call x1, Pallas kernels: 80.7 us -> 75.1 us  [fused(): pl.pallas_call(kernel, out_shape=jax.ShapeDtypeStruct((examples, queries....]
where the time goes in v3:
time: 76.5 us; the launch traced here: 76.3 us
  Pallas kernels  75.1 us (98%)
  local copies, waits for them, and re-layouts  1.26 us (2%)
    pallas_call x1, Pallas kernels, fused(): pl.pallas_call(kernel, out_shape=jax.ShapeDtypeStruct((examples, queries....  75.1 us

profile of v3, /device:TPU:0, one launch (start us, length us, event | category | flops | bytes accessed | tf_op | source)
XLA Modules:
  0.0 76.3 jit_solution(5216660207906163304)
XLA Ops:
  0.0 75.1 %shard_map.100 = f32[4,128]{1,0:T(4,128)} custom-call(bf16[512,1792]{1,0:T(8,128)(2,1)} %gate_h.1, bf16[512,1792]{1,0:T(8,128)(2,1)} %up_h.1, bf16[32,8192]{1,0:T(8,128)(2,1)} %og_h.1, bf16[512,512]{1,0:T(8,128)(2,1)} %li_h.1, bf16[1792,8192]{1,0:T(8,128)(2,1)} %w_h.1, bf16[64,1792]{1,0:T(8,128)(2,1)} %pid_h.1, bf16[64,8192]{1,0:T(8,128)(2,1)} %pod_h.1, ...), custom_call_target="tpu_custom_call" | custom-call | flops 15032385536 | bytes 29360128 | tf_op jit(solution)/shard_map/pallas_call | solution.py:371
  75.1 1.3 %copy.12 = f32[4,128]{1,0:T(4,128)} copy(f32[4,128]{1,0:T(4,128)} %shard_map.100) | data formatting | bytes 4096
